TPU v7x, 128 devices: a whole 4x4x4 slice. The times are simulated.
128 devices in a mesh: row: 4 (over y_hi, core), col: 8 (over y_lo, z), depth: 4 (over x).
Axes of the slice: x: 4, y: 4 (y_hi: 2, y_lo: 2; y = y_hi * 2 + y_lo), z: 4, core: 2. Of those that a mesh axis runs over, the one named last changes fastest.
Arguments:
- out_factor: bfloat16 [8192, 8192], P('row', ('depth', 'col')), may hold values from -1 to 4
- gradient: bfloat16 [8192, 8192], P(('depth', 'row'), 'col'), may hold values from -6 to 6
- in_factor: bfloat16 [8192, 8192], P('col', ('row', 'depth')), may hold values from -1 to 4
Outputs:
- update: float32 [8192, 8192], P(('row', 'depth'), 'col')
All inputs are finite; a program needn't handle non-finite values.
Results may differ from a plain program's by a relative error of at most 0.0029.
Values may be sent and summed in bfloat16 or wider, within the bound.
A program may use at most 128 MiB of HBM per device.

v0:
```python
import jax
import jax.numpy as jnp
from jax import lax
from jax.sharding import PartitionSpec as P


def shards(out_factor, gradient, in_factor):
    col_count = lax.axis_size("col")
    depth_count = lax.axis_size("depth")
    row_count = lax.axis_size("row")
    own_rows = lax.all_to_all(out_factor, "depth", split_axis=0, concat_axis=1, tiled=True)
    factor_rows = lax.all_gather(own_rows, "col", axis=1, tiled=True)
    row_total = factor_rows.shape[0]
    factor_rows = factor_rows.reshape(row_total, col_count, depth_count, -1)
    factor_rows = factor_rows.transpose(0, 2, 1, 3).reshape(row_total, depth_count, row_count, -1)
    grad_whole = lax.all_gather(gradient, ("row", "depth"), axis=0, tiled=True)
    grad_whole = grad_whole.reshape(row_count, depth_count, -1, gradient.shape[1])
    hidden_sum = jnp.einsum(
        "rdqt,qdtj->rj", factor_rows, grad_whole, preferred_element_type=jnp.float32
    )
    hidden = hidden_sum.astype(jnp.bfloat16)
    partial_terms = jnp.dot(
        hidden,
        lax.all_gather(in_factor, ("row", "depth"), axis=1, tiled=True),
        preferred_element_type=jnp.float32,
    )
    return lax.psum_scatter(partial_terms, "col", scatter_dimension=1, tiled=True)


def solution(mesh):
    in_specs = (P("row", ("depth", "col")), P(("depth", "row"), "col"), P("col", ("row", "depth")))
    out_specs = P(("row", "depth"), "col")
    return jax.shard_map(shards, mesh=mesh, in_specs=in_specs, out_specs=out_specs, check_vma=False)
```

profile of v0, /device:TPU:1, one launch (start us, length us, event | category | flops | bytes accessed | tf_op | source)
XLA Modules:
  0.0 547.6 jit_solution(10613743627860165896)
XLA Ops:
  6.5 0.0 all-gather.4.cloned.1.call-start
  6.5 19.0 %all_to_all.19 = bf16[4,512,256]{2,1,0:T(8,128)(2,1)S(1)} all-to-all(bf16[4,512,256]{2,1,0:T(8,128)(2,1)} %bitcast.19), channel_id=1, replica_groups=mesh['row'=4,'col'=8,'depth'=4] {'depth'}, dimensions={0} | all-to-all | bytes 2097152 | tf_op jit(solution)/shard_map/all_to_all | solution.py:11
  25.6 1.3 copy.8
  26.9 0.0 all-gather.4.cloned.1.call-update
  26.9 0.0 all-gather.6.cloned.1.call-start
  27.0 0.7 all-gather.6.cloned.1.call-update
  27.7 0.0 all-gather.8.cloned.1.call-start
  27.7 0.7 all-gather.8.cloned.1.call-update
  28.4 0.0 reduce-scatter.2.cloned.1.call-start
  28.4 92.5 %all-gather.4.cloned.1.call-done = bf16[512,8192]{0,1:T(8,128)(2,1)} async-done(((bf16[512,1024]{0,1:T(8,128)(2,1)}), bf16[512,8192]{0,1:T(8,128)(2,1)}) %all-gather.4.cloned.1.call-update) | async-done | bytes 8388624 | tf_op jit(solution)/shard_map/all_gather | solution.py:12
  120.9 7.5 %copy.9 = bf16[512,8,4,256]{0,3,1,2:T(8,128)(2,1)} copy(bf16[512,8,4,256]{0,3,2,1:T(8,128)(2,1)} %bitcast.15) | data formatting | bytes 16777216 | tf_op jit(solution)/shard_map/reshape | solution.py:14
  128.4 104.3 %all-gather.6.cloned.1.call-done = bf16[8192,1024]{1,0:T(8,128)(2,1)} async-done(((bf16[512,1024]{1,0:T(8,128)(2,1)}), bf16[8192,1024]{1,0:T(8,128)(2,1)}) %all-gather.6.cloned.1.call-update) | async-done | bytes 16777232 | tf_op jit(solution)/shard_map/all_gather | solution.py:16
  232.7 14.8 %bitcast_convert_fusion = bf16[512,1024]{1,0:T(8,128)(2,1)S(1)} fusion(bf16[512,4,4,512]{0,3,2,1:T(8,128)(2,1)} %bitcast.16, bf16[4,4,512,1024]{3,2,1,0:T(8,128)(2,1)} %bitcast.20), kind=kOutput, calls=%fused_computation.2 | convolution fusion | flops 8590458880 | bytes 26214400 | tf_op jit(solution)/shard_map/rdqt,qdtj->rj/dot_general | solution.py:18
  247.5 108.5 %all-gather.8.cloned.1.call-done = bf16[1024,8192]{1,0:T(8,128)(2,1)} async-done(((bf16[1024,512]{1,0:T(8,128)(2,1)}), bf16[1024,8192]{1,0:T(8,128)(2,1)}) %all-gather.8.cloned.1.call-update) | async-done | bytes 16777232 | tf_op jit(solution)/shard_map/all_gather | solution.py:24
  356.0 15.6 %fusion.4 = f32[512,8192]{1,0:T(8,128)} fusion(bf16[512,1024]{1,0:T(8,128)(2,1)S(1)} %bitcast_convert_fusion, bf16[1024,8192]{1,0:T(8,128)(2,1)} %all-gather.8.cloned.1.call-done), kind=kOutput, calls=%fused_computation.3 | convolution fusion | flops 8589934592 | bytes 34603008 | tf_op jit(solution)/shard_map/dot_general | solution.py:22
  371.6 0.0 reduce-scatter.2.cloned.1.call-update
  371.6 169.4 %reduce-scatter.2.cloned.1.call-done = f32[512,1024]{1,0:T(8,128)} async-done(((f32[512,8192]{1,0:T(8,128)}), f32[512,1024]{1,0:T(8,128)}) %reduce-scatter.2.cloned.1.call-update) | async-done | bytes 2097168 | tf_op jit(solution)/shard_map/reduce_scatter | solution.py:27
Async XLA Ops:
  6.5 114.4 %all-gather.4.cloned.1.call-start = ((), (), s32[]{:S(2)}) async-start(), calls=%async_computation.2 | async-start | bytes 9437184 | tf_op jit(solution)/shard_map/all_gather | solution.py:12
  26.9 205.8 %all-gather.6.cloned.1.call-start = ((), (), s32[]{:S(2)}) async-start(), calls=%async_computation.3 | async-start | bytes 17825792 | tf_op jit(solution)/shard_map/all_gather | solution.py:16
  27.7 328.3 %all-gather.8.cloned.1.call-start = ((), (), s32[]{:S(2)}) async-start(), calls=%async_computation.4 | async-start | bytes 17825792 | tf_op jit(solution)/shard_map/all_gather | solution.py:24
  28.4 512.7 %reduce-scatter.2.cloned.1.call-start = ((), (), s32[]{:S(2)}) async-start(), calls=%async_computation.5 | async-start | bytes 18874368 | tf_op jit(solution)/shard_map/reduce_scatter | solution.py:27
Sparse Core Ops, SparseCore 0:
  27.0 93.8 all-gather.3
  123.4 109.2 all-gather.5
  234.9 120.9 all-gather.7
  371.8 169.2 reduce-scatter.1
where the time goes:
time: 548 us
  waiting for transfers between devices  476 us (87%)
  matrix products  30.5 us (6%)
  blocking collectives  19 us (3%)
  between operations  13.1 us (2%)
  local copies, waits for them, and re-layouts  8.79 us (2%)
    reduce_scatter x1, waiting for transfers between devices, shards(): lax.psum_scatter(partial_terms, 'col', scatter_dimension=1, tiled=True)  169 us
    all_gather x1, waiting for transfers between devices, shards(): lax.all_gather(in_factor, ('row', 'depth'), axis=1, tiled=True)  108 us
    all_gather x1, waiting for transfers between devices, shards(): grad_whole = lax.all_gather(gradient, ('row', 'depth'), axis=0, tiled=True)  104 us
    all_gather x1, waiting for transfers between devices, shards(): factor_rows = lax.all_gather(own_rows, 'col', axis=1, tiled=True)  92.5 us
    all_to_all x1, blocking collectives, shards(): lax.all_to_all(out_factor, 'depth', split_axis=0, concat_axis=1, tiled=True)  19 us
    dot_general x1, matrix products, shards(): jnp.dot(hidden, lax.all_gather(in_factor, ('row', 'depth'), axis=1, tiled...  15.6 us
    dot_general x1, matrix products, shards(): jnp.einsum('rdqt,qdtj->rj', factor_rows, grad_whole, preferred_element_ty...  14.8 us
  transfers between devices with their start and end apart: 4, of which 4 were waited for; matrix products, arithmetic and copies ran while one was open for 4% of the time, Pallas kernels for 0%

commit v1 on v0

v1 whole, which is shorter than its diff:
```python
import jax
import jax.numpy as jnp
from jax import lax
from jax.sharding import PartitionSpec as P


def shards(out_factor, gradient, in_factor):
    rows, cols = lax.axis_size("row"), lax.axis_size("col")
    pair = cols // rows
    factor_block = lax.all_gather(out_factor, "col", axis=1, tiled=True)
    grad_block = lax.all_gather(gradient, "row", axis=0, tiled=True)
    terms = jnp.dot(factor_block, grad_block, preferred_element_type=jnp.float32)
    hidden = lax.psum_scatter(terms, "depth", scatter_dimension=0, tiled=True).astype(jnp.bfloat16)
    hidden_rows = lax.all_gather(hidden, "row", axis=0, tiled=True)
    in_block = lax.all_gather(in_factor, "depth", axis=1, tiled=True)
    partial_terms = jnp.dot(hidden_rows, in_block, preferred_element_type=jnp.float32)
    height, width = hidden.shape
    chunks = partial_terms.reshape(rows, height, pair, width).transpose(0, 2, 1, 3).reshape(cols * height, width)
    summed = lax.psum_scatter(chunks, "col", scatter_dimension=0, tiled=True)
    moves = [
        (row * cols + to_row * pair + part, to_row * cols + row * pair + part)
        for row in range(rows)
        for to_row in range(rows)
        for part in range(pair)
    ]
    return lax.ppermute(summed, ("row", "col"), moves)


def solution(mesh):
    in_specs = (P("row", ("depth", "col")), P(("depth", "row"), "col"), P("col", ("row", "depth")))
    out_specs = P(("row", "depth"), "col")
    return jax.shard_map(shards, mesh=mesh, in_specs=in_specs, out_specs=out_specs, check_vma=False)
```

time: 548 us -> 618 us (1.13)
  the two profiles are of different devices: /device:TPU:1 before, /device:TPU:16 now
where the time goes in v1:
time: 618 us; the launch traced here: 617 us
  waiting for transfers between devices  530 us (86%)
  local copies, waits for them, and re-layouts  39.1 us (6%)
  matrix products  29.5 us (5%)
  between operations  13.5 us (2%)
    reduce_scatter x1, waiting for transfers between devices, shards(): summed = lax.psum_scatter(chunks, 'col', scatter_dimension=0, tiled=True)  174 us
    all_gather x1, waiting for transfers between devices, shards(): factor_block = lax.all_gather(out_factor, 'col', axis=1, tiled=True)  102 us
    reduce_scatter x1, waiting for transfers between devices, shards(): lax.psum_scatter(terms, 'depth', scatter_dimension=0, tiled=True)  81.1 us
    ppermute x1, waiting for transfers between devices, shards(): return lax.ppermute(summed, ('row', 'col'), moves)  48.4 us
    all_gather x1, waiting for transfers between devices, shards(): in_block = lax.all_gather(in_factor, 'depth', axis=1, tiled=True)  46.7 us
    all_gather x1, waiting for transfers between devices, shards(): grad_block = lax.all_gather(gradient, 'row', axis=0, tiled=True)  39 us
    all_gather x1, waiting for transfers between devices, shards(): hidden_rows = lax.all_gather(hidden, 'row', axis=0, tiled=True)  37.7 us
    reshape x1, local copies, waits for them, and re-layouts, shards(): partial_terms.reshape(rows, height, pair, width).transpose(0, 2, 1, 3)  22 us
  transfers between devices with their start and end apart: 7, of which 7 were waited for; matrix products, arithmetic and copies ran while one was open for 0% of the time, Pallas kernels for 0%

profile of v1, /device:TPU:16, one launch (start us, length us, event | category | flops | bytes accessed | tf_op | source)
XLA Modules:
  0.0 617.3 jit_solution(6219064349219297561)
XLA Ops:
  6.5 0.7 all-gather.7.cloned.1.call-update
  7.3 0.0 all-gather.5.cloned.1.call-start
  7.3 0.7 all-gather.5.cloned.1.call-update
  8.0 0.0 reduce-scatter.3.cloned.1.call-start
  8.1 39.0 %all-gather.7.cloned.1.call-done = bf16[2048,1024]{1,0:T(8,128)(2,1)} async-done(((bf16[512,1024]{1,0:T(8,128)(2,1)}), bf16[2048,1024]{1,0:T(8,128)(2,1)}) %all-gather.7.cloned.1.call-update) | async-done | bytes 4194320 | tf_op jit(solution)/shard_map/all_gather | solution.py:11
  47.1 101.9 %all-gather.5.cloned.1.call-done = bf16[2048,2048]{1,0:T(8,128)(2,1)} async-done(((bf16[2048,256]{1,0:T(8,128)(2,1)}), bf16[2048,2048]{1,0:T(8,128)(2,1)}) %all-gather.5.cloned.1.call-update) | async-done | bytes 8388624 | tf_op jit(solution)/shard_map/all_gather | solution.py:10
  149.0 14.4 %fusion = f32[2048,1024]{1,0:T(8,128)} fusion(bf16[2048,2048]{1,0:T(8,128)(2,1)} %all-gather.5.cloned.1.call-done, bf16[2048,1024]{1,0:T(8,128)(2,1)} %all-gather.7.cloned.1.call-done), kind=kOutput, calls=%fused_computation | convolution fusion | flops 8589934592 | bytes 20971520 | tf_op jit(solution)/shard_map/dot_general | solution.py:12
  163.4 0.0 all-gather.11.cloned.1.call-start
  163.5 0.5 all-gather.11.cloned.1.call-update
  164.0 0.0 all-gather.9.cloned.1.call-start
  164.0 81.1 %reduce-scatter.3.cloned.1.call-done = f32[512,1024]{1,0:T(8,128)} async-done(((f32[2048,1024]{1,0:T(8,128)}), f32[512,1024]{1,0:T(8,128)}) %reduce-scatter.3.cloned.1.call-update) | async-done | bytes 2097168 | tf_op jit(solution)/shard_map/reduce_scatter | solution.py:13
  245.2 2.7 convert_element_type.3
  247.9 0.0 all-gather.9.cloned.1.call-update
  247.9 0.0 reduce-scatter.5.cloned.1.call-start
  248.0 46.7 %all-gather.11.cloned.1.call-done = bf16[1024,2048]{1,0:T(8,128)(2,1)} async-done(((bf16[1024,512]{1,0:T(8,128)(2,1)}), bf16[1024,2048]{1,0:T(8,128)(2,1)}) %all-gather.11.cloned.1.call-update) | async-done | bytes 4194320 | tf_op jit(solution)/shard_map/all_gather | solution.py:15
  294.7 37.7 %all-gather.9.cloned.1.call-done = bf16[2048,1024]{1,0:T(8,128)(2,1)} async-done(((bf16[512,1024]{1,0:T(8,128)(2,1)}), bf16[2048,1024]{1,0:T(8,128)(2,1)}) %all-gather.9.cloned.1.call-update) | async-done | bytes 4194320 | tf_op jit(solution)/shard_map/all_gather | solution.py:14
  332.4 15.1 %fusion.1 = f32[2048,2048]{1,0:T(8,128)} fusion(bf16[2048,1024]{1,0:T(8,128)(2,1)} %all-gather.9.cloned.1.call-done, bf16[1024,2048]{1,0:T(8,128)(2,1)} %all-gather.11.cloned.1.call-done), kind=kOutput, calls=%fused_computation.1 | convolution fusion | flops 8589934592 | bytes 25165824 | tf_op jit(solution)/shard_map/dot_general | solution.py:16
  347.5 22.0 %reshape.6 = f32[4,512,2,1024]{3,2,1,0:T(2,128)} reshape(f32[2048,2048]{1,0:T(8,128)} %fusion.1) | data formatting | bytes 33554432 | tf_op jit(solution)/shard_map/reshape | solution.py:18
  369.5 15.8 %copy.4 = f32[4,2,512,1024]{3,2,1,0:T(8,128)} copy(f32[4,2,512,1024]{3,1,2,0:T(2,128)} %bitcast.7) | data formatting | bytes 33554432 | tf_op jit(solution)/shard_map/transpose | solution.py:18
  385.3 0.0 reduce-scatter.5.cloned.1.call-update
  385.4 173.5 %reduce-scatter.5.cloned.1.call-done = f32[512,1024]{1,0:T(8,128)} async-done(((f32[4096,1024]{1,0:T(8,128)}), f32[512,1024]{1,0:T(8,128)}) %reduce-scatter.5.cloned.1.call-update) | async-done | bytes 2097168 | tf_op jit(solution)/shard_map/reduce_scatter | solution.py:19
  558.9 1.9 collective-permute-start
  560.8 48.4 %collective-permute-done = f32[512,1024]{1,0:T(8,128)S(1)} collective-permute-done((f32[512,1024]{1,0:T(8,128)}, f32[512,1024]{1,0:T(8,128)S(1)}, u32[]{:S(2)}, u32[]{:S(2)}) %collective-permute-start) | collective-permute-done | bytes 2097184 | tf_op jit(solution)/shard_map/ppermute | solution.py:26
  609.2 1.3 copy.6
  (2 shorter events, 0.0 us)
Async XLA Ops:
  6.5 40.5 %all-gather.7.cloned.1.call-start = ((), (), s32[]{:S(2)}) async-start(), calls=%async_computation.3 | async-start | bytes 5242880 | tf_op jit(solution)/shard_map/all_gather | solution.py:11
  7.3 141.7 %all-gather.5.cloned.1.call-start = ((), (), s32[]{:S(2)}) async-start(), calls=%async_computation.2 | async-start | bytes 9437184 | tf_op jit(solution)/shard_map/all_gather | solution.py:10
  8.0 237.2 %reduce-scatter.3.cloned.1.call-start = ((), (), s32[]{:S(2)}) async-start(), calls=%async_computation.4 | async-start | bytes 10485760 | tf_op jit(solution)/shard_map/reduce_scatter | solution.py:13
  163.4 131.3 %all-gather.11.cloned.1.call-start = ((), (), s32[]{:S(2)}) async-start(), calls=%async_computation.6 | async-start | bytes 5242880 | tf_op jit(solution)/shard_map/all_gather | solution.py:15
  164.0 168.4 %all-gather.9.cloned.1.call-start = ((), (), s32[]{:S(2)}) async-start(), calls=%async_computation.5 | async-start | bytes 5242880 | tf_op jit(solution)/shard_map/all_gather | solution.py:14
  247.9 311.0 %reduce-scatter.5.cloned.1.call-start = ((), (), s32[]{:S(2)}) async-start(), calls=%async_computation.7 | async-start | bytes 18874368 | tf_op jit(solution)/shard_map/reduce_scatter | solution.py:19
  558.9 50.3 %collective-permute-start = (f32[512,1024]{1,0:T(8,128)}, f32[512,1024]{1,0:T(8,128)S(1)}, u32[]{:S(2)}, u32[]{:S(2)}) collective-permute-start(f32[512,1024]{1,0:T(8,128)} %reduce-scatter.5.cloned.1.call-done), channel_id=1, source_target_pairs={{0,0},{4,4},{8,32},{12,36},{16,64},{20,68},{24,96},{28,100},{32,8}... | collective-permute-start | bytes 6291464 | tf_op jit(solution)/shard_map/ppermute | solution.py:26
Sparse Core Ops, SparseCore 0:
  9.0 37.9 all-gather.6
  48.6 100.2 all-gather.4
  163.5 81.6 reduce-scatter.2
  246.7 47.9 all-gather.10
  296.2 36.1 all-gather.8
  385.5 173.3 reduce-scatter.4

commit v2 on v1

v2 whole, which is shorter than its diff:
```python
import functools
import jax
import jax.numpy as jnp
from jax import lax
from jax.experimental import pallas as pl
from jax.experimental.pallas import tpu as pltpu
from jax.sharding import PartitionSpec as P

MESH = pl.DeviceIdType.MESH
BF16 = jnp.bfloat16
F32 = jnp.float32
PARTS = 2
TILE = 256


def place(x, y, z, core):
    return ((y // 2) * 2 + core, (y % 2) * 4 + z, x)


def kernel(a_in, g_in, b_in, out, a_all, g_all, b_all, terms, terms_in, own_h, h_all, u_out, u_in,
           swap_s, swap_r, az_s, az_r, ac_s, ac_r, g_s, g_r, turn_s, turn_r, bx_s, bx_r, bc_s, bc_r,
           t_s, t_r, h_s, h_r, u_s, u_r):
    row, col, x = lax.axis_index("row"), lax.axis_index("col"), lax.axis_index("depth")
    y_hi, core, y_lo, z = row // 2, row % 2, col // 4, col % 4
    y = y_hi * 2 + y_lo
    other = 1 - core
    sibling = place(x, y, z, other)
    straight = core == y_lo
    height = own_h.shape[0]
    part = height // PARTS

    def remote(src, dst, send, recv, to):
        return pltpu.make_async_remote_copy(
            src_ref=src, dst_ref=dst, send_sem=send, recv_sem=recv, device_id=to, device_id_type=MESH
        )

    barrier = pltpu.get_barrier_semaphore()
    partners = [sibling]
    for step in range(1, 4):
        partners.append(place(x, (y + step) % 4, z, 0))
        partners.append(place(x, (y + step) % 4, z, 1))
        partners.append(place(x, y, (z + step) % 4, core))
        partners.append(place((x + step) % 4, y, z, core))
        partners.append(place(x, (y + 2) % 4, (z + step) % 4, core))
    for partner in partners:
        pl.semaphore_signal(barrier, inc=1, device_id=partner, device_id_type=MESH)
    pl.semaphore_wait(barrier, len(partners))

    def span(index):
        return pl.ds(index * part, part)

    mine_a = core * 4 + z
    swapped = place(x, y_hi * 2 + core, z, y_lo)

    def swap(p):
        src, dst = a_in.at[:, span(p), :], a_all.at[mine_a, :, span(p), :]
        to_slot = a_all.at[y_lo * 4 + z, :, span(p), :]
        return (
            remote(src, to_slot, swap_s.at[p], swap_r.at[p], swapped),
            pltpu.make_async_copy(src, dst, swap_r.at[p]),
        )

    def swap_start(p):
        away, here = swap(p)

        @pl.when(straight)
        def _():
            here.start()

        @pl.when(jnp.logical_not(straight))
        def _():
            away.start()

    def swap_wait(p):
        src, dst = a_in.at[:, span(p), :], a_all.at[mine_a, :, span(p), :]

        @pl.when(straight)
        def _():
            pltpu.make_async_copy(src, dst, swap_r.at[p]).wait()

        @pl.when(jnp.logical_not(straight))
        def _():
            arrived = remote(src, dst, swap_s.at[p], swap_r.at[p], swapped)
            arrived.wait_recv()
            arrived.wait_send()

    def along_z(p, step):
        ref = a_all.at[mine_a, :, span(p), :]
        return remote(ref, ref, az_s.at[p, step - 1], az_r.at[p, step - 1], place(x, y, (z + step) % 4, core))

    def along_z_wait(p, step):
        ref = a_all.at[core * 4 + (z + 4 - step) % 4, :, span(p), :]
        remote(ref, ref, az_s.at[p, step - 1], az_r.at[p, step - 1], sibling).wait_recv()

    def across_a(p, step):
        ref = a_all.at[core * 4 + (z + 4 - step) % 4, :, span(p), :]
        return remote(ref, ref, ac_s.at[p, step], ac_r.at[p, step], sibling)

    def across_a_wait(p, step):
        ref = a_all.at[other * 4 + (z + 4 - step) % 4, :, span(p), :]
        remote(ref, ref, ac_s.at[p, step], ac_r.at[p, step], sibling).wait_recv()

    def spread_start(src, dst, send, recv):
        for step in (2, 1, 3):
            remote(src, dst, send.at[step], recv.at[row], place(x, (y + step) % 4, z, y_lo)).start()

        @pl.when(straight)
        def _():
            pltpu.make_async_copy(src, dst, recv.at[row]).start()

        @pl.when(jnp.logical_not(straight))
        def _():
            remote(src, dst, send.at[0], recv.at[row], sibling).start()

    def spread_sent(src, dst, send, recv):
        for step in (1, 2, 3):
            remote(src, dst, send.at[step], recv.at[row], sibling).wait_send()

        @pl.when(jnp.logical_not(straight))
        def _():
            remote(src, dst, send.at[0], recv.at[row], sibling).wait_send()

    def spread_wait(slots, send, recv):
        for slot in range(4):
            local = jnp.logical_and(straight, row == slot)

            @pl.when(local)
            def _():
                pltpu.make_async_copy(slots(slot), slots(slot), recv.at[slot]).wait()

            @pl.when(jnp.logical_not(local))
            def _():
                remote(slots(slot), slots(slot), send.at[0], recv.at[slot], sibling).wait_recv()

    turned = place(x, core * 2 + y_hi, z, y_lo)
    still = jnp.logical_and(y_hi == y_lo, y_lo == core)

    def turn_start():
        @pl.when(still)
        def _():
            pltpu.make_async_copy(b_in, b_all.at[core, x], turn_r).start()

        @pl.when(jnp.logical_not(still))
        def _():
            remote(b_in, b_all.at[y_lo, x], turn_s, turn_r, turned).start()

    def turn_wait():
        @pl.when(still)
        def _():
            pltpu.make_async_copy(b_in, b_all.at[core, x], turn_r).wait()

        @pl.when(jnp.logical_not(still))
        def _():
            arrived = remote(b_in, b_all.at[core, x], turn_s, turn_r, turned)
            arrived.wait_recv()
            arrived.wait_send()

    def along_x(step):
        ref = b_all.at[core, x]
        return remote(ref, ref, bx_s.at[step - 1], bx_r.at[step - 1], place((x + step) % 4, y, z, core))

    def along_x_wait(step):
        ref = b_all.at[core, (x + 4 - step) % 4]
        remote(ref, ref, bx_s.at[step - 1], bx_r.at[step - 1], sibling).wait_recv()

    def across_b(step):
        ref = b_all.at[core, (x + 4 - step) % 4]
        return remote(ref, ref, bc_s.at[step], bc_r.at[step], sibling)

    def across_b_wait(step):
        ref = b_all.at[other, (x + 4 - step) % 4]
        remote(ref, ref, bc_s.at[step], bc_r.at[step], sibling).wait_recv()

    def give(p, step):
        return remote(
            terms.at[step, span(p), :], terms_in.at[step - 1, span(p), :], t_s.at[p, step - 1], t_r.at[p, step - 1],
            place((x + step) % 4, y, z, core),
        )

    def update_to(p, upper, half):
        return remote(
            u_out.at[upper, half, span(p), :], u_in.at[z, span(p), :], u_s.at[p, upper, half], u_r.at[p, z],
            place(x, upper * 2 + y_lo, y_hi * 2 + half, core),
        )

    def is_own(upper, half):
        return jnp.logical_and(upper == y_hi, y_hi * 2 + half == z)

    for p in range(PARTS):
        swap_start(p)
    spread_start(g_in, g_all.at[row], g_s, g_r)
    turn_start()
    for p in range(PARTS):
        swap_wait(p)
        for step in (2, 1, 3):
            along_z(p, step).start()
        across_a(p, 0).start()
    turn_wait()
    for step in (2, 1, 3):
        along_x(step).start()
    across_b(0).start()

    def first_product(p, step):
        owner = (x + step) % 4

        def tile(index, _):
            columns = pl.ds(pl.multiple_of(index * TILE, TILE), TILE)
            left = jnp.concatenate([a_all[slot, owner, span(p), :] for slot in range(8)], axis=1)
            right = jnp.concatenate([g_all[slot, :, columns] for slot in range(4)], axis=0)
            terms[step, span(p), columns] = jnp.dot(left, right, preferred_element_type=F32)
            return 0

        lax.fori_loop(0, own_h.shape[1] // TILE, tile, 0)

    def second_product(p, upper, half):
        def tile(index, _):
            columns = pl.ds(pl.multiple_of((index % 2) * TILE, TILE), TILE)
            left = jnp.concatenate([h_all[upper * 2 + slot, span(p), :] for slot in range(2)], axis=1)
            right = jnp.concatenate([b_all[slot, half * 2 + index // 2, :, columns] for slot in range(2)], axis=0)
            target = pl.ds(pl.multiple_of(index * TILE, TILE), TILE)
            u_out[upper, half, span(p), target] = jnp.dot(left, right, preferred_element_type=F32).astype(BF16)
            return 0

        lax.fori_loop(0, own_h.shape[1] // TILE, tile, 0)

    for p in range(PARTS):
        for step in (1, 3, 2):
            along_z_wait(p, step)
            across_a(p, step).start()
        if p == 0:
            spread_wait(lambda slot: g_all.at[slot], g_s, g_r)
        for step in range(4):
            across_a_wait(p, step)
        for step in (2, 1, 3):
            first_product(p, step)
            give(p, step).start()
        first_product(p, 0)

    for step in (1, 3, 2):
        along_x_wait(step)
        across_b(step).start()

    for p in range(PARTS):
        for step in (1, 3, 2):
            give(p, step).wait_recv()
        total = terms[0, span(p), :]
        for step in range(3):
            total += terms_in[step, span(p), :]
        own_h[span(p), :] = total.astype(BF16)
        spread_start(own_h.at[span(p), :], h_all.at[row, span(p), :], h_s.at[p], h_r.at[p])

    for step in range(4):
        across_b_wait(step)
    for p in range(PARTS):
        spread_wait(lambda slot: h_all.at[slot, span(p), :], h_s.at[p], h_r.at[p])
        for upper in range(2):
            for half in range(2):
                second_product(p, upper, half)
                own = is_own(upper, half)

                @pl.when(own)
                def _():
                    pltpu.make_async_copy(
                        u_out.at[upper, half, span(p), :], u_in.at[z, span(p), :], u_r.at[p, z]
                    ).start()

                @pl.when(jnp.logical_not(own))
                def _():
                    update_to(p, upper, half).start()

    for p in range(PARTS):
        for source in range(4):
            ref = u_in.at[source, span(p), :]
            local = jnp.logical_and(source == z, y_hi == z // 2)

            @pl.when(local)
            def _():
                pltpu.make_async_copy(ref, ref, u_r.at[p, source]).wait()

            @pl.when(jnp.logical_not(local))
            def _():
                remote(ref, ref, u_s.at[p, 0, 0], u_r.at[p, source], sibling).wait_recv()

        total = u_in[0, span(p), :].astype(F32)
        for source in range(1, 4):
            total += u_in[source, span(p), :].astype(F32)
        out[span(p), :] = total

    spread_sent(g_in, g_all.at[row], g_s, g_r)
    for step in (1, 2, 3):
        along_x(step).wait_send()
    for step in range(4):
        across_b(step).wait_send()
    for p in range(PARTS):
        for step in (1, 2, 3):
            along_z(p, step).wait_send()
            give(p, step).wait_send()
        for step in range(4):
            across_a(p, step).wait_send()
        spread_sent(own_h.at[span(p), :], h_all.at[row, span(p), :], h_s.at[p], h_r.at[p])
        for upper in range(2):
            for half in range(2):
                @pl.when(jnp.logical_not(is_own(upper, half)))
                def _():
                    update_to(p, upper, half).wait_send()


def shards(out_factor, gradient, in_factor):
    height, width = gradient.shape
    dma = pltpu.SemaphoreType.DMA
    return pl.pallas_call(
        kernel,
        out_shape=jax.ShapeDtypeStruct((height, width), F32),
        in_specs=[pl.BlockSpec(memory_space=pl.ANY)] * 3,
        out_specs=pl.BlockSpec(memory_space=pltpu.VMEM),
        scratch_shapes=[
            pltpu.VMEM((8, 4, height, out_factor.shape[1]), BF16),
            pltpu.VMEM((4, height, width), BF16),
            pltpu.VMEM((2, 4) + in_factor.shape, BF16),
            pltpu.VMEM((4, height, width), F32),
            pltpu.VMEM((3, height, width), F32),
            pltpu.VMEM((height, width), BF16),
            pltpu.VMEM((4, height, width), BF16),
            pltpu.VMEM((2, 2, height, width), BF16),
            pltpu.VMEM((4, height, width), BF16),
            dma((PARTS,)), dma((PARTS,)),
            dma((PARTS, 3)), dma((PARTS, 3)),
            dma((PARTS, 4)), dma((PARTS, 4)),
            dma((4,)), dma((4,)),
            dma, dma,
            dma((3,)), dma((3,)),
            dma((4,)), dma((4,)),
            dma((PARTS, 3)), dma((PARTS, 3)),
            dma((PARTS, 4)), dma((PARTS, 4)),
            dma((PARTS, 2, 2)), dma((PARTS, 4)),
        ],
        compiler_params=pltpu.CompilerParams(
            collective_id=0, has_side_effects=True, vmem_limit_bytes=60 * 2**20
        ),
        cost_estimate=pl.CostEstimate(flops=2 * 2**34, bytes_accessed=8 * 2**20, transcendentals=0),
    )(out_factor.reshape(4, height, -1), gradient, in_factor)


def solution(mesh):
    in_specs = (P("row", ("depth", "col")), P(("depth", "row"), "col"), P("col", ("row", "depth")))
    out_specs = P(("row", "depth"), "col")
    return jax.shard_map(shards, mesh=mesh, in_specs=in_specs, out_specs=out_specs, check_vma=False)
```

time: 618 us -> 322 us (0.52)
  the two profiles are of different devices: /device:TPU:16 before, /device:TPU:59 now
where the time goes in v2:
time: 322 us
  Pallas kernels  319 us (99%)
    pallas_call x1, Pallas kernels, shards(): pl.pallas_call(kernel, out_shape=jax.ShapeDtypeStruct((height, width), F3...  319 us

profile of v2, /device:TPU:59, one launch (start us, length us, event | category | flops | bytes accessed | tf_op | source)
XLA Modules:
  0.0 321.7 jit_solution(268705410247692229)
XLA Ops:
  0.0 318.6 %shard_map.37 = f32[512,1024]{1,0:T(8,128)} custom-call(bf16[4,512,256]{2,1,0:T(8,128)(2,1)} %bitcast.1, bf16[512,1024]{1,0:T(8,128)(2,1)} %g_in.1, bf16[1024,512]{1,0:T(8,128)(2,1)} %b_in.1), custom_call_target="tpu_custom_call" | custom-call | flops 34359738368 | bytes 8388608 | tf_op jit(solution)/shard_map/pallas_call | solution.py:311
  318.6 3.2 copy.5

commit v3 on v2

v3 whole, which is shorter than its diff:
```python
import functools
import jax
import jax.numpy as jnp
from jax import lax
from jax.experimental import pallas as pl
from jax.experimental.pallas import tpu as pltpu
from jax.sharding import PartitionSpec as P

MESH = pl.DeviceIdType.MESH
BF16 = jnp.bfloat16
F32 = jnp.float32
PARTS = 4
LOADS = 2
SIDES = 2
TILE = 256


def place(x, y, z, core):
    return ((y // 2) * 2 + core, (y % 2) * 4 + z, x)


def kernel(a_in, g_in, b_in, out, a_all, g_all, b_all, terms, terms_in, far, far_in, own_h, h_all, u_out, u_in,
           swap_s, swap_r, az_s, az_r, ac_s, ac_r, g_s, g_r, turn_s, turn_r, bx_s, bx_r, bc_s, bc_r,
           t_s, t_r, h_s, h_r, u_s, u_r):
    row, col, x = lax.axis_index("row"), lax.axis_index("col"), lax.axis_index("depth")
    y_hi, core, y_lo, z = row // 2, row % 2, col // 4, col % 4
    y = y_hi * 2 + y_lo
    other = 1 - core
    sibling = place(x, y, z, other)
    straight = core == y_lo
    height = own_h.shape[0]
    part = height // PARTS
    load = height // LOADS
    side = own_h.shape[1] // SIDES
    quarter = b_in.shape[1]

    def remote(src, dst, send, recv, to):
        return pltpu.make_async_remote_copy(
            src_ref=src, dst_ref=dst, send_sem=send, recv_sem=recv, device_id=to, device_id_type=MESH
        )

    barrier = pltpu.get_barrier_semaphore()
    partners = [sibling]
    for step in range(1, 4):
        partners.append(place(x, (y + step) % 4, z, 0))
        partners.append(place(x, (y + step) % 4, z, 1))
        partners.append(place(x, y, (z + step) % 4, core))
        partners.append(place((x + step) % 4, y, z, core))
        partners.append(place(x, (y + 2) % 4, (z + step) % 4, core))
    for partner in partners:
        pl.semaphore_signal(barrier, inc=1, device_id=partner, device_id_type=MESH)
    pl.semaphore_wait(barrier, len(partners))

    def span(index):
        return pl.ds(index * part, part)

    def rows_of(index):
        return pl.ds(index * load, load)

    def half_of(index):
        return pl.ds(index * side, side)

    mine_a = core * 4 + z
    swapped = place(x, y_hi * 2 + core, z, y_lo)

    def swap(p):
        src, dst = a_in.at[:, rows_of(p), :], a_all.at[mine_a, :, rows_of(p), :]
        to_slot = a_all.at[y_lo * 4 + z, :, rows_of(p), :]
        return (
            remote(src, to_slot, swap_s.at[p], swap_r.at[p], swapped),
            pltpu.make_async_copy(src, dst, swap_r.at[p]),
        )

    def swap_start(p):
        away, here = swap(p)

        @pl.when(straight)
        def _():
            here.start()

        @pl.when(jnp.logical_not(straight))
        def _():
            away.start()

    def swap_wait(p):
        src, dst = a_in.at[:, rows_of(p), :], a_all.at[mine_a, :, rows_of(p), :]

        @pl.when(straight)
        def _():
            pltpu.make_async_copy(src, dst, swap_r.at[p]).wait()

        @pl.when(jnp.logical_not(straight))
        def _():
            arrived = remote(src, dst, swap_s.at[p], swap_r.at[p], swapped)
            arrived.wait_recv()
            arrived.wait_send()

    def along_z(p, step):
        ref = a_all.at[mine_a, :, rows_of(p), :]
        return remote(ref, ref, az_s.at[p, step - 1], az_r.at[p, step - 1], place(x, y, (z + step) % 4, core))

    def along_z_wait(p, step):
        ref = a_all.at[core * 4 + (z + 4 - step) % 4, :, rows_of(p), :]
        remote(ref, ref, az_s.at[p, step - 1], az_r.at[p, step - 1], sibling).wait_recv()

    def across_a(p, step):
        ref = a_all.at[core * 4 + (z + 4 - step) % 4, :, rows_of(p), :]
        return remote(ref, ref, ac_s.at[p, step], ac_r.at[p, step], sibling)

    def across_a_wait(p, step):
        ref = a_all.at[other * 4 + (z + 4 - step) % 4, :, rows_of(p), :]
        remote(ref, ref, ac_s.at[p, step], ac_r.at[p, step], sibling).wait_recv()

    def spread_start(src, dst, send, recv):
        for step in (2, 1, 3):
            remote(src, dst, send.at[step], recv.at[row], place(x, (y + step) % 4, z, y_lo)).start()

        @pl.when(straight)
        def _():
            pltpu.make_async_copy(src, dst, recv.at[row]).start()

        @pl.when(jnp.logical_not(straight))
        def _():
            remote(src, dst, send.at[0], recv.at[row], sibling).start()

    def spread_sent(src, dst, send, recv):
        for step in (1, 2, 3):
            remote(src, dst, send.at[step], recv.at[row], sibling).wait_send()

        @pl.when(jnp.logical_not(straight))
        def _():
            remote(src, dst, send.at[0], recv.at[row], sibling).wait_send()

    def spread_wait(slots, send, recv):
        for slot in range(4):
            local = jnp.logical_and(straight, row == slot)

            @pl.when(local)
            def _():
                pltpu.make_async_copy(slots(slot), slots(slot), recv.at[slot]).wait()

            @pl.when(jnp.logical_not(local))
            def _():
                remote(slots(slot), slots(slot), send.at[0], recv.at[slot], sibling).wait_recv()

    odd = x % 2
    turned = place(x, ((core + odd) % 2) * 2 + y_hi, z, y_lo)
    still = jnp.logical_and(jnp.logical_and(y_hi == y_lo, y_lo == core), odd == 0)

    def turn_start():
        @pl.when(still)
        def _():
            pltpu.make_async_copy(b_in, b_all.at[core, x], turn_r).start()

        @pl.when(jnp.logical_not(still))
        def _():
            remote(b_in, b_all.at[y_lo, x], turn_s, turn_r, turned).start()

    def turn_wait():
        @pl.when(still)
        def _():
            pltpu.make_async_copy(b_in, b_all.at[core, x], turn_r).wait()

        @pl.when(jnp.logical_not(still))
        def _():
            arrived = remote(b_in, b_all.at[core, x], turn_s, turn_r, turned)
            arrived.wait_recv()
            arrived.wait_send()

    def along_x(step):
        ref = b_all.at[core, x]
        return remote(ref, ref, bx_s.at[step - 1], bx_r.at[step - 1], place((x + step) % 4, y, z, core))

    def along_x_wait(step):
        ref = b_all.at[core, (x + 4 - step) % 4]
        remote(ref, ref, bx_s.at[step - 1], bx_r.at[step - 1], sibling).wait_recv()

    def across_b(step):
        ref = b_all.at[core, (x + 4 - step) % 4]
        return remote(ref, ref, bc_s.at[step], bc_r.at[step], sibling)

    def across_b_wait(step):
        ref = b_all.at[other, (x + 4 - step) % 4]
        remote(ref, ref, bc_s.at[step], bc_r.at[step], sibling).wait_recv()

    def give(p, j, step):
        block = (span(p), half_of(j))
        if step == 2:
            src, dst = far.at[block], far_in.at[block]
        else:
            src, dst = terms.at[(step // 2 + 1,) + block], terms_in.at[(step // 2,) + block]
        return remote(src, dst, t_s.at[p, j, step - 1], t_r.at[p, j, step - 1], place((x + step) % 4, y, z, core))

    def owner_z(block):
        return ((y_hi + block) % 2) * 2 + block // 2

    def update_refs(p, upper, block):
        return (
            u_out.at[upper, span(p), pl.ds(block * quarter, quarter)],
            u_in.at[z, span(p), pl.ds((block % 2) * quarter, quarter)],
        )

    def update_to(p, upper, block):
        src, dst = update_refs(p, upper, block)
        return remote(
            src, dst, u_s.at[p, upper, block], u_r.at[p, z, block % 2],
            place(x, upper * 2 + y_lo, owner_z(block), core),
        )

    def is_own(upper, block):
        return jnp.logical_and(upper == y_hi, owner_z(block) == z)

    for p in range(LOADS):
        swap_start(p)
    turn_start()
    for p in range(LOADS):
        swap_wait(p)
        for step in (2, 1, 3):
            along_z(p, step).start()
        across_a(p, 0).start()
    turn_wait()
    for step in (2, 1, 3):
        along_x(step).start()
    across_b(0).start()
    for j in range(SIDES):
        spread_start(g_in.at[:, half_of(j)], g_all.at[row, :, half_of(j)], g_s.at[j], g_r.at[j])

    def first_product(p, j, step):
        owner = (x + step) % 4

        def tile(index, _):
            columns = pl.ds(pl.multiple_of(j * side + index * TILE, TILE), TILE)
            left = jnp.concatenate([a_all[slot, owner, span(p), :] for slot in range(8)], axis=1)
            right = jnp.concatenate([g_all[slot, :, columns] for slot in range(4)], axis=0)
            product = jnp.dot(left, right, preferred_element_type=F32)
            if step == 2:
                far[span(p), columns] = product.astype(BF16)
            else:
                terms[(step + 1) // 2, span(p), columns] = product
            return 0

        lax.fori_loop(0, side // TILE, tile, 0)

    def second_product(p, upper, block):
        def tile(index, _):
            columns = pl.ds(pl.multiple_of(index * TILE, TILE), TILE)
            left = jnp.concatenate([h_all[upper * 2 + slot, span(p), :] for slot in range(2)], axis=1)
            right = jnp.concatenate([b_all[slot, block, :, columns] for slot in range(2)], axis=0)
            target = pl.ds(pl.multiple_of(block * quarter + index * TILE, TILE), TILE)
            u_out[upper, span(p), target] = jnp.dot(left, right, preferred_element_type=F32).astype(BF16)
            return 0

        lax.fori_loop(0, quarter // TILE, tile, 0)

    def arrive_a(p):
        for step in (1, 3, 2):
            along_z_wait(p, step)
            across_a(p, step).start()
        for step in range(4):
            across_a_wait(p, step)

    def arrive_g(j):
        spread_wait(lambda slot: g_all.at[slot, :, half_of(j)], g_s.at[j], g_r.at[j])

    def send_terms(p, j):
        for step in (2, 1, 3):
            first_product(p, j, step)
            give(p, j, step).start()
        first_product(p, j, 0)

    arrive_a(0)
    arrive_g(0)
    for p in range(PARTS // 2):
        send_terms(p, 0)
    for step in (1, 3, 2):
        along_x_wait(step)
        across_b(step).start()
    arrive_a(1)
    arrive_g(1)
    for p in range(PARTS // 2):
        send_terms(p, 1)
    for p in range(PARTS // 2, PARTS):
        for j in range(SIDES):
            send_terms(p, j)

    for p in range(PARTS):
        for j in range(SIDES):
            for step in (1, 3, 2):
                give(p, j, step).wait_recv()
        total = terms[0, span(p), :] + far_in[span(p), :].astype(F32)
        for step in range(2):
            total += terms_in[step, span(p), :]
        own_h[span(p), :] = total.astype(BF16)
        spread_start(own_h.at[span(p), :], h_all.at[row, span(p), :], h_s.at[p], h_r.at[p])

    for step in range(4):
        across_b_wait(step)
    for p in range(PARTS):
        spread_wait(lambda slot: h_all.at[slot, span(p), :], h_s.at[p], h_r.at[p])
        for upper in range(2):
            for block in range(4):
                second_product(p, upper, block)
                own = is_own(upper, block)

                @pl.when(own)
                def _():
                    src, dst = update_refs(p, upper, block)
                    pltpu.make_async_copy(src, dst, u_r.at[p, z, block % 2]).start()

                @pl.when(jnp.logical_not(own))
                def _():
                    update_to(p, upper, block).start()

    for p in range(PARTS):
        for source in range(4):
            for half in range(2):
                ref = u_in.at[source, span(p), pl.ds(half * quarter, quarter)]
                local = jnp.logical_and(source == z, (z // 2 + half) % 2 == y_hi)

                @pl.when(local)
                def _():
                    pltpu.make_async_copy(ref, ref, u_r.at[p, source, half]).wait()

                @pl.when(jnp.logical_not(local))
                def _():
                    remote(ref, ref, u_s.at[p, 0, 0], u_r.at[p, source, half], sibling).wait_recv()

        total = u_in[0, span(p), :].astype(F32)
        for source in range(1, 4):
            total += u_in[source, span(p), :].astype(F32)
        out[span(p), :] = total

    for j in range(SIDES):
        spread_sent(g_in.at[:, half_of(j)], g_all.at[row, :, half_of(j)], g_s.at[j], g_r.at[j])
    for step in (1, 2, 3):
        along_x(step).wait_send()
    for step in range(4):
        across_b(step).wait_send()
    for p in range(LOADS):
        for step in (1, 2, 3):
            along_z(p, step).wait_send()
        for step in range(4):
            across_a(p, step).wait_send()
    for p in range(PARTS):
        for j in range(SIDES):
            for step in (1, 2, 3):
                give(p, j, step).wait_send()
        spread_sent(own_h.at[span(p), :], h_all.at[row, span(p), :], h_s.at[p], h_r.at[p])
        for upper in range(2):
            for block in range(4):
                @pl.when(jnp.logical_not(is_own(upper, block)))
                def _():
                    update_to(p, upper, block).wait_send()


def shards(out_factor, gradient, in_factor):
    height, width = gradient.shape
    dma = pltpu.SemaphoreType.DMA
    return pl.pallas_call(
        kernel,
        out_shape=jax.ShapeDtypeStruct((height, width), F32),
        in_specs=[pl.BlockSpec(memory_space=pl.ANY)] * 3,
        out_specs=pl.BlockSpec(memory_space=pltpu.VMEM),
        scratch_shapes=[
            pltpu.VMEM((8, 4, height, out_factor.shape[1]), BF16),
            pltpu.VMEM((4, height, width), BF16),
            pltpu.VMEM((2, 4) + in_factor.shape, BF16),
            pltpu.VMEM((3, height, width), F32),
            pltpu.VMEM((2, height, width), F32),
            pltpu.VMEM((height, width), BF16),
            pltpu.VMEM((height, width), BF16),
            pltpu.VMEM((height, width), BF16),
            pltpu.VMEM((4, height, width), BF16),
            pltpu.VMEM((2, height, 2 * width), BF16),
            pltpu.VMEM((4, height, width), BF16),
            dma((LOADS,)), dma((LOADS,)),
            dma((LOADS, 3)), dma((LOADS, 3)),
            dma((LOADS, 4)), dma((LOADS, 4)),
            dma((SIDES, 4)), dma((SIDES, 4)),
            dma, dma,
            dma((3,)), dma((3,)),
            dma((4,)), dma((4,)),
            dma((PARTS, SIDES, 3)), dma((PARTS, SIDES, 3)),
            dma((PARTS, 4)), dma((PARTS, 4)),
            dma((PARTS, 2, 4)), dma((PARTS, 4, 2)),
        ],
        compiler_params=pltpu.CompilerParams(
            collective_id=0, has_side_effects=True, vmem_limit_bytes=60 * 2**20
        ),
        cost_estimate=pl.CostEstimate(flops=2 * 2**34, bytes_accessed=8 * 2**20, transcendentals=0),
    )(out_factor.reshape(4, height, -1), gradient, in_factor)


def solution(mesh):
    in_specs = (P("row", ("depth", "col")), P(("depth", "row"), "col"), P("col", ("row", "depth")))
    out_specs = P(("row", "depth"), "col")
    return jax.shard_map(shards, mesh=mesh, in_specs=in_specs, out_specs=out_specs, check_vma=False)
```

time: 322 us -> 215 us (0.67)
  the two profiles are of different devices: /device:TPU:59 before, /device:TPU:1 now
where the time goes in v3:
time: 215 us; the launch traced here: 214 us
  Pallas kernels  211 us (98%)
  local copies, waits for them, and re-layouts  3.16 us (1%)
    pallas_call x1, Pallas kernels, shards(): pl.pallas_call(kernel, out_shape=jax.ShapeDtypeStruct((height, width), F3...  211 us

profile of v3, /device:TPU:1, one launch (start us, length us, event | category | flops | bytes accessed | tf_op | source)
XLA Modules:
  0.0 214.4 jit_solution(17224390502990825482)
XLA Ops:
  0.0 211.2 %shard_map.37 = f32[512,1024]{1,0:T(8,128)} custom-call(bf16[4,512,256]{2,1,0:T(8,128)(2,1)} %bitcast.1, bf16[512,1024]{1,0:T(8,128)(2,1)} %g_in.1, bf16[1024,512]{1,0:T(8,128)(2,1)} %b_in.1), custom_call_target="tpu_custom_call" | custom-call | flops 34359738368 | bytes 8388608 | tf_op jit(solution)/shard_map/pallas_call | solution.py:359
  211.3 3.2 %copy.5 = f32[512,1024]{1,0:T(8,128)} copy(f32[512,1024]{1,0:T(8,128)} %shard_map.37) | data formatting | bytes 4194304

commit v4 on v3

--- a/solution.py
+++ b/solution.py
@@ -12,16 +12,16 @@
 PARTS = 4
 LOADS = 2
 SIDES = 2
-TILE = 256
+TILE = 512
 
 
 def place(x, y, z, core):
     return ((y // 2) * 2 + core, (y % 2) * 4 + z, x)
 
 
-def kernel(a_in, g_in, b_in, out, a_all, g_all, b_all, terms, terms_in, far, far_in, own_h, h_all, u_out, u_in,
+def kernel(a_in, g_in, b_in, out, a_all, g_all, b_all, terms, terms_in, far, far_in, own_h, h_all, u_out, u_own, u_in, cross_out, cross_in,
            swap_s, swap_r, az_s, az_r, ac_s, ac_r, g_s, g_r, turn_s, turn_r, bx_s, bx_r, bc_s, bc_r,
-           t_s, t_r, h_s, h_r, u_s, u_r):
+           t_s, t_r, h_s, h_r, u_s, u_r, c_s, c_r):
     row, col, x = lax.axis_index("row"), lax.axis_index("col"), lax.axis_index("depth")
     y_hi, core, y_lo, z = row // 2, row % 2, col // 4, col % 4
     y = y_hi * 2 + y_lo
@@ -46,7 +46,6 @@
         partners.append(place(x, (y + step) % 4, z, 1))
         partners.append(place(x, y, (z + step) % 4, core))
         partners.append(place((x + step) % 4, y, z, core))
-        partners.append(place(x, (y + 2) % 4, (z + step) % 4, core))
     for partner in partners:
         pl.semaphore_signal(barrier, inc=1, device_id=partner, device_id_type=MESH)
     pl.semaphore_wait(barrier, len(partners))
@@ -147,33 +146,49 @@
     turned = place(x, ((core + odd) % 2) * 2 + y_hi, z, y_lo)
     still = jnp.logical_and(jnp.logical_and(y_hi == y_lo, y_lo == core), odd == 0)
 
-    def turn_start():
+    def b_rows(index):
+        return pl.ds(index * (b_in.shape[0] // 2), b_in.shape[0] // 2)
+
+    def turn_start(bit):
+        src, dst = b_in.at[b_rows(bit), :], b_all.at[core, x, b_rows(bit), :]
+
         @pl.when(still)
         def _():
-            pltpu.make_async_copy(b_in, b_all.at[core, x], turn_r).start()
+            pltpu.make_async_copy(src, dst, turn_r.at[bit]).start()
 
         @pl.when(jnp.logical_not(still))
         def _():
-            remote(b_in, b_all.at[y_lo, x], turn_s, turn_r, turned).start()
-
-    def turn_wait():
+            to_slot = b_all.at[y_lo, x, b_rows(bit), :]
+            remote(src, to_slot, turn_s.at[bit], turn_r.at[bit], turned).start()
+
+    def turn_wait(bit):
+        src, dst = b_in.at[b_rows(bit), :], b_all.at[core, x, b_rows(bit), :]
+
         @pl.when(still)
         def _():
-            pltpu.make_async_copy(b_in, b_all.at[core, x], turn_r).wait()
+            pltpu.make_async_copy(src, dst, turn_r.at[bit]).wait()
 
         @pl.when(jnp.logical_not(still))
         def _():
-            arrived = remote(b_in, b_all.at[core, x], turn_s, turn_r, turned)
+            arrived = remote(src, dst, turn_s.at[bit], turn_r.at[bit], turned)
             arrived.wait_recv()
             arrived.wait_send()
 
-    def along_x(step):
-        ref = b_all.at[core, x]
-        return remote(ref, ref, bx_s.at[step - 1], bx_r.at[step - 1], place((x + step) % 4, y, z, core))
-
-    def along_x_wait(step):
-        ref = b_all.at[core, (x + 4 - step) % 4]
-        remote(ref, ref, bx_s.at[step - 1], bx_r.at[step - 1], sibling).wait_recv()
+    def along_x(step, part):
+        ref = b_all.at[core, x, b_rows(part), :]
+        return remote(ref, ref, bx_s.at[step // 2, part], bx_r.at[step // 2, part], place((x + step) % 4, y, z, core))
+
+    def along_x_wait(step, part):
+        ref = b_all.at[core, (x + 4 - step) % 4, b_rows(part), :]
+        remote(ref, ref, bx_s.at[step // 2, part], bx_r.at[step // 2, part], sibling).wait_recv()
+
+    def pass_x(step, part):
+        ref = b_all.at[core, (x + 4 - step) % 4, b_rows(part), :]
+        return remote(ref, ref, bx_s.at[2, part], bx_r.at[2, part], place((x + step) % 4, y, z, core))
+
+    def pass_x_wait(part):
+        ref = b_all.at[core, (x + 2) % 4, b_rows(part), :]
+        remote(ref, ref, bx_s.at[2, part], bx_r.at[2, part], sibling).wait_recv()
 
     def across_b(step):
         ref = b_all.at[core, (x + 4 - step) % 4]
@@ -186,41 +201,39 @@
     def give(p, j, step):
         block = (span(p), half_of(j))
         if step == 2:
-            src, dst = far.at[block], far_in.at[block]
+            src, dst, to = far.at[block], far_in.at[block], relay(j)
         else:
-            src, dst = terms.at[(step // 2 + 1,) + block], terms_in.at[(step // 2,) + block]
-        return remote(src, dst, t_s.at[p, j, step - 1], t_r.at[p, j, step - 1], place((x + step) % 4, y, z, core))
-
-    def owner_z(block):
-        return ((y_hi + block) % 2) * 2 + block // 2
-
-    def update_refs(p, upper, block):
-        return (
-            u_out.at[upper, span(p), pl.ds(block * quarter, quarter)],
-            u_in.at[z, span(p), pl.ds((block % 2) * quarter, quarter)],
+            src, dst, to = terms.at[(step // 2 + 1,) + block], terms_in.at[(step // 2,) + block], step
+        return remote(src, dst, t_s.at[p, j, step - 1], t_r.at[p, j, step - 1], place((x + to) % 4, y, z, core))
+
+    def relay(j):
+        return 1 if j == 0 else 3
+
+    def block_of(owner):
+        return (owner % 2) * 2 + (owner // 2 + y_hi) % 2
+
+    def update_to(p, away, step):
+        return remote(
+            u_out.at[step - 1, away, span(p), :], u_in.at[step - 1, away, span(p), :],
+            u_s.at[p, away, step - 1], u_r.at[p, away, step - 1], place(x, y, (z + step) % 4, core),
         )
 
-    def update_to(p, upper, block):
-        src, dst = update_refs(p, upper, block)
+    def cross(p):
         return remote(
-            src, dst, u_s.at[p, upper, block], u_r.at[p, z, block % 2],
-            place(x, upper * 2 + y_lo, owner_z(block), core),
+            cross_out.at[span(p), :], cross_in.at[span(p), :], c_s.at[p], c_r.at[p], place(x, (y + 2) % 4, z, core)
         )
 
-    def is_own(upper, block):
-        return jnp.logical_and(upper == y_hi, owner_z(block) == z)
-
     for p in range(LOADS):
+        turn_start(p)
         swap_start(p)
-    turn_start()
     for p in range(LOADS):
+        turn_wait(p)
+        for step in (1, 3):
+            along_x(step, p).start()
         swap_wait(p)
         for step in (2, 1, 3):
             along_z(p, step).start()
         across_a(p, 0).start()
-    turn_wait()
-    for step in (2, 1, 3):
-        along_x(step).start()
     across_b(0).start()
     for j in range(SIDES):
         spread_start(g_in.at[:, half_of(j)], g_all.at[row, :, half_of(j)], g_s.at[j], g_r.at[j])
@@ -235,22 +248,32 @@
             product = jnp.dot(left, right, preferred_element_type=F32)
             if step == 2:
                 far[span(p), columns] = product.astype(BF16)
+            elif step == relay(j):
+                terms[(step + 1) // 2, span(p), columns] = product + far_in[span(p), columns].astype(F32)
             else:
                 terms[(step + 1) // 2, span(p), columns] = product
             return 0
 
         lax.fori_loop(0, side // TILE, tile, 0)
 
-    def second_product(p, upper, block):
-        def tile(index, _):
-            columns = pl.ds(pl.multiple_of(index * TILE, TILE), TILE)
-            left = jnp.concatenate([h_all[upper * 2 + slot, span(p), :] for slot in range(2)], axis=1)
-            right = jnp.concatenate([b_all[slot, block, :, columns] for slot in range(2)], axis=0)
-            target = pl.ds(pl.multiple_of(block * quarter + index * TILE, TILE), TILE)
-            u_out[upper, span(p), target] = jnp.dot(left, right, preferred_element_type=F32).astype(BF16)
-            return 0
-
-        lax.fori_loop(0, quarter // TILE, tile, 0)
+    def second_product(p, away, step):
+        upper = (y_hi + away) % 2
+        block = block_of((z + step) % 4)
+        left = jnp.concatenate([h_all[upper * 2 + slot, span(p), :] for slot in range(2)], axis=1)
+        right = jnp.concatenate([b_all[slot, block] for slot in range(2)], axis=0)
+        product = jnp.dot(left, right, preferred_element_type=F32)
+        if step == 0:
+            u_own[away, span(p), :] = product
+        else:
+            u_out[step - 1, away, span(p), :] = product.astype(BF16)
+
+    def share_b():
+        for step, bit in ((1, 1), (3, 0)):
+            along_x_wait(step, bit)
+            across_b(step).start()
+        for bit in range(2):
+            pass_x_wait(bit)
+        across_b(2).start()
 
     def arrive_a(p):
         for step in (1, 3, 2):
@@ -262,78 +285,102 @@
     def arrive_g(j):
         spread_wait(lambda slot: g_all.at[slot, :, half_of(j)], g_s.at[j], g_r.at[j])
 
-    def send_terms(p, j):
-        for step in (2, 1, 3):
+    def send_far(p, j):
+        first_product(p, j, 2)
+        give(p, j, 2).start()
+
+    def send_near(p, j):
+        for step in (4 - relay(j), relay(j)):
+            if step == relay(j):
+                give(p, j, 2).wait_recv()
             first_product(p, j, step)
             give(p, j, step).start()
         first_product(p, j, 0)
 
-    arrive_a(0)
-    arrive_g(0)
-    for p in range(PARTS // 2):
-        send_terms(p, 0)
-    for step in (1, 3, 2):
-        along_x_wait(step)
-        across_b(step).start()
-    arrive_a(1)
-    arrive_g(1)
-    for p in range(PARTS // 2):
-        send_terms(p, 1)
-    for p in range(PARTS // 2, PARTS):
+    def send_terms(chunks):
+        send_far(*chunks[0])
+        for now, later in zip(chunks, chunks[1:] + [None]):
+            if later is not None:
+                send_far(*later)
+            send_near(*now)
+
+    def sum_terms(p):
         for j in range(SIDES):
-            send_terms(p, j)
-
-    for p in range(PARTS):
-        for j in range(SIDES):
-            for step in (1, 3, 2):
+            for step in (1, 3):
                 give(p, j, step).wait_recv()
-        total = terms[0, span(p), :] + far_in[span(p), :].astype(F32)
+        total = terms[0, span(p), :]
         for step in range(2):
             total += terms_in[step, span(p), :]
         own_h[span(p), :] = total.astype(BF16)
         spread_start(own_h.at[span(p), :], h_all.at[row, span(p), :], h_s.at[p], h_r.at[p])
 
+    arrive_a(0)
+    for step, bit in ((1, 0), (3, 1)):
+        along_x_wait(step, bit)
+        pass_x(step, bit).start()
+    arrive_g(0)
+    early = list(range(PARTS // 2))
+    send_terms([(p, 0) for p in early])
+    arrive_a(1)
+    arrive_g(1)
+    def send_update(p):
+        spread_wait(lambda slot: h_all.at[slot, span(p), :], h_s.at[p], h_r.at[p])
+        for away in (1, 0):
+            for step in (2, 1, 3):
+                second_product(p, away, step)
+                update_to(p, away, step).start()
+            second_product(p, away, 0)
+
+    def sum_update(p, away):
+        for step in (1, 3, 2):
+            update_to(p, away, step).wait_recv()
+        total = u_own[away, span(p), :]
+        for step in range(3):
+            total += u_in[step, away, span(p), :].astype(F32)
+        return total
+
+    half = (z // 2 + y_hi) % 2
+
+    def place_update(p):
+        cross_out[span(p), :] = sum_update(p, 1)
+        cross(p).start()
+        out[span(p), pl.ds(pl.multiple_of(half * quarter, quarter), quarter)] = sum_update(p, 0)
+
+    send_far(0, 1)
+    send_far(1, 1)
+    send_near(0, 1)
+    send_far(2, 0)
+    send_near(1, 1)
+    share_b()
+    send_far(2, 1)
+    send_near(2, 0)
+    sum_terms(0)
+    send_far(3, 0)
+    send_near(2, 1)
+    sum_terms(1)
+    send_far(3, 1)
+    send_near(3, 0)
+    send_near(3, 1)
+    sum_terms(2)
     for step in range(4):
         across_b_wait(step)
     for p in range(PARTS):
-        spread_wait(lambda slot: h_all.at[slot, span(p), :], h_s.at[p], h_r.at[p])
-        for upper in range(2):
-            for block in range(4):
-                second_product(p, upper, block)
-                own = is_own(upper, block)
-
-                @pl.when(own)
-                def _():
-                    src, dst = update_refs(p, upper, block)
-                    pltpu.make_async_copy(src, dst, u_r.at[p, z, block % 2]).start()
-
-                @pl.when(jnp.logical_not(own))
-                def _():
-                    update_to(p, upper, block).start()
-
+        send_update(p)
+        if p == 0:
+            sum_terms(3)
+        if p >= 1:
+            place_update(p - 1)
+    place_update(PARTS - 1)
     for p in range(PARTS):
-        for source in range(4):
-            for half in range(2):
-                ref = u_in.at[source, span(p), pl.ds(half * quarter, quarter)]
-                local = jnp.logical_and(source == z, (z // 2 + half) % 2 == y_hi)
-
-                @pl.when(local)
-                def _():
-                    pltpu.make_async_copy(ref, ref, u_r.at[p, source, half]).wait()
-
-                @pl.when(jnp.logical_not(local))
-                def _():
-                    remote(ref, ref, u_s.at[p, 0, 0], u_r.at[p, source, half], sibling).wait_recv()
-
-        total = u_in[0, span(p), :].astype(F32)
-        for source in range(1, 4):
-            total += u_in[source, span(p), :].astype(F32)
-        out[span(p), :] = total
+        cross(p).wait_recv()
+        out[span(p), pl.ds(pl.multiple_of((1 - half) * quarter, quarter), quarter)] = cross_in[span(p), :]
 
     for j in range(SIDES):
         spread_sent(g_in.at[:, half_of(j)], g_all.at[row, :, half_of(j)], g_s.at[j], g_r.at[j])
-    for step in (1, 2, 3):
-        along_x(step).wait_send()
+    for step in (1, 3):
+        for bit in range(2):
+            along_x(step, bit).wait_send()
+        pass_x(step, step // 2).wait_send()
     for step in range(4):
         across_b(step).wait_send()
     for p in range(LOADS):
@@ -346,11 +393,10 @@
             for step in (1, 2, 3):
                 give(p, j, step).wait_send()
         spread_sent(own_h.at[span(p), :], h_all.at[row, span(p), :], h_s.at[p], h_r.at[p])
-        for upper in range(2):
-            for block in range(4):
-                @pl.when(jnp.logical_not(is_own(upper, block)))
-                def _():
-                    update_to(p, upper, block).wait_send()
+        for away in range(2):
+            for step in (1, 2, 3):
+                update_to(p, away, step).wait_send()
+        cross(p).wait_send()
 
 
 def shards(out_factor, gradient, in_factor):
@@ -371,18 +417,22 @@
             pltpu.VMEM((height, width), BF16),
             pltpu.VMEM((height, width), BF16),
             pltpu.VMEM((4, height, width), BF16),
-            pltpu.VMEM((2, height, 2 * width), BF16),
-            pltpu.VMEM((4, height, width), BF16),
+            pltpu.VMEM((3, 2, height, in_factor.shape[1]), BF16),
+            pltpu.VMEM((2, height, in_factor.shape[1]), F32),
+            pltpu.VMEM((3, 2, height, in_factor.shape[1]), BF16),
+            pltpu.VMEM((height, in_factor.shape[1]), F32),
+            pltpu.VMEM((height, in_factor.shape[1]), F32),
             dma((LOADS,)), dma((LOADS,)),
             dma((LOADS, 3)), dma((LOADS, 3)),
             dma((LOADS, 4)), dma((LOADS, 4)),
             dma((SIDES, 4)), dma((SIDES, 4)),
-            dma, dma,
-            dma((3,)), dma((3,)),
+            dma((2,)), dma((2,)),
+            dma((3, 2)), dma((3, 2)),
             dma((4,)), dma((4,)),
             dma((PARTS, SIDES, 3)), dma((PARTS, SIDES, 3)),
             dma((PARTS, 4)), dma((PARTS, 4)),
-            dma((PARTS, 2, 4)), dma((PARTS, 4, 2)),
+            dma((PARTS, 2, 3)), dma((PARTS, 2, 3)),
+            dma((PARTS,)), dma((PARTS,)),
         ],
         compiler_params=pltpu.CompilerParams(
             collective_id=0, has_side_effects=True, vmem_limit_bytes=60 * 2**20

time: 215 us -> 183 us (0.85); the launches traced: 214 us -> 180 us
  Pallas kernels: 211 us -> 177 us
    pallas_call x1, Pallas kernels: 211 us -> 177 us  [shards(): pl.pallas_call(kernel, out_shape=jax.ShapeDtypeStruct((height, width), F3...]
where the time goes in v4:
time: 183 us; the launch traced here: 180 us
  Pallas kernels  177 us (97%)
  local copies, waits for them, and re-layouts  3.16 us (2%)
    pallas_call x1, Pallas kernels, shards(): pl.pallas_call(kernel, out_shape=jax.ShapeDtypeStruct((height, width), F3...  177 us

profile of v4, /device:TPU:1, one launch (start us, length us, event | category | flops | bytes accessed | tf_op | source)
XLA Modules:
  0.0 180.0 jit_solution(624001379596296439)
XLA Ops:
  0.0 176.9 %shard_map.37 = f32[512,1024]{1,0:T(8,128)} custom-call(bf16[4,512,256]{2,1,0:T(8,128)(2,1)} %bitcast.1, bf16[512,1024]{1,0:T(8,128)(2,1)} %g_in.1, bf16[1024,512]{1,0:T(8,128)(2,1)} %b_in.1), custom_call_target="tpu_custom_call" | custom-call | flops 34359738368 | bytes 8388608 | tf_op jit(solution)/shard_map/pallas_call | solution.py:405
  176.9 3.2 %copy.5 = f32[512,1024]{1,0:T(8,128)} copy(f32[512,1024]{1,0:T(8,128)} %shard_map.37) | data formatting | bytes 4194304

commit v5 on v4

--- a/solution.py
+++ b/solution.py
@@ -20,7 +20,7 @@
 
 
 def kernel(a_in, g_in, b_in, out, a_all, g_all, b_all, terms, terms_in, far, far_in, own_h, h_all, u_out, u_own, u_in, cross_out, cross_in,
-           swap_s, swap_r, az_s, az_r, ac_s, ac_r, g_s, g_r, turn_s, turn_r, bx_s, bx_r, bc_s, bc_r,
+           swap_s, swap_r, az_s, az_r, ac_s, ac_r, g_s, g_r, f_s, turn_s, turn_r, bx_s, bx_r, bc_s, bc_r,
            t_s, t_r, h_s, h_r, u_s, u_r, c_s, c_r):
     row, col, x = lax.axis_index("row"), lax.axis_index("col"), lax.axis_index("depth")
     y_hi, core, y_lo, z = row // 2, row % 2, col // 4, col % 4
@@ -141,6 +141,85 @@
             @pl.when(jnp.logical_not(local))
             def _():
                 remote(slots(slot), slots(slot), send.at[0], recv.at[slot], sibling).wait_recv()
+
+    def g_block(slot, j, bit):
+        tall = g_in.shape[0] // 2
+        return g_all.at[slot, pl.ds(bit * tall, tall), half_of(j)]
+
+    def g_copy(j, bit, step):
+        tall = g_in.shape[0] // 2
+        to = sibling if step == 0 else place(x, (y + step) % 4, z, y_lo)
+        return remote(
+            g_in.at[pl.ds(bit * tall, tall), half_of(j)], g_block(row, j, bit),
+            g_s.at[j, bit, step // 2 + (step > 0)], g_r.at[j, row, bit], to,
+        )
+
+    def g_start(j):
+        for step, bit in ((1, 0), (3, 1), (1, 1), (3, 0)):
+            g_copy(j, bit, step).start()
+        for bit in range(2):
+            @pl.when(straight)
+            def _():
+                src = g_in.at[pl.ds(bit * (g_in.shape[0] // 2), g_in.shape[0] // 2), half_of(j)]
+                pltpu.make_async_copy(src, g_block(row, j, bit), g_r.at[j, row, bit]).start()
+
+            @pl.when(jnp.logical_not(straight))
+            def _():
+                g_copy(j, bit, 0).start()
+
+    def g_sent(j):
+        for bit in range(2):
+            for step in (1, 3):
+                g_copy(j, bit, step).wait_send()
+
+            @pl.when(jnp.logical_not(straight))
+            def _():
+                g_copy(j, bit, 0).wait_send()
+
+    def g_slot(step, which):
+        return ((y + step) % 4) // 2 * 2 + which
+
+    def g_pass(j, which, step):
+        ref = g_block(g_slot(4 - step, which), j, step // 2)
+        return remote(
+            ref, ref, f_s.at[j, which, step // 2], g_r.at[j, g_slot(4 - step, which), step // 2],
+            place(x, (y + step) % 4, z, core),
+        )
+
+    def g_got(slot, j, bit):
+        ref = g_block(slot, j, bit)
+        remote(ref, ref, g_s.at[j, bit, 0], g_r.at[j, slot, bit], sibling).wait_recv()
+
+    def g_relay(j):
+        @pl.when(jnp.logical_not(straight))
+        def _():
+            for step in (1, 3):
+                for which in range(2):
+                    g_got(g_slot(4 - step, which), j, step // 2)
+                    g_pass(j, which, step).start()
+
+    def g_relayed(j):
+        @pl.when(jnp.logical_not(straight))
+        def _():
+            for step in (1, 3):
+                for which in range(2):
+                    g_pass(j, which, step).wait_send()
+
+    def arrive_g(j):
+        @pl.when(straight)
+        def _():
+            for bit in range(2):
+                own = g_block(row, j, bit)
+                pltpu.make_async_copy(own, own, g_r.at[j, row, bit]).wait()
+                g_got(g_slot(0, other), j, bit)
+                for which in range(2):
+                    g_got(g_slot(2, which), j, bit)
+
+        @pl.when(jnp.logical_not(straight))
+        def _():
+            for step in (1, 3):
+                for which in range(2):
+                    g_got(g_slot(4 - step, which), j, 1 - step // 2)
 
     odd = x % 2
     turned = place(x, ((core + odd) % 2) * 2 + y_hi, z, y_lo)
@@ -236,7 +315,7 @@
         across_a(p, 0).start()
     across_b(0).start()
     for j in range(SIDES):
-        spread_start(g_in.at[:, half_of(j)], g_all.at[row, :, half_of(j)], g_s.at[j], g_r.at[j])
+        g_start(j)
 
     def first_product(p, j, step):
         owner = (x + step) % 4
@@ -282,9 +361,6 @@
         for step in range(4):
             across_a_wait(p, step)
 
-    def arrive_g(j):
-        spread_wait(lambda slot: g_all.at[slot, :, half_of(j)], g_s.at[j], g_r.at[j])
-
     def send_far(p, j):
         first_product(p, j, 2)
         give(p, j, 2).start()
@@ -314,10 +390,12 @@
         own_h[span(p), :] = total.astype(BF16)
         spread_start(own_h.at[span(p), :], h_all.at[row, span(p), :], h_s.at[p], h_r.at[p])
 
+    g_relay(0)
     arrive_a(0)
     for step, bit in ((1, 0), (3, 1)):
         along_x_wait(step, bit)
         pass_x(step, bit).start()
+    g_relay(1)
     arrive_g(0)
     early = list(range(PARTS // 2))
     send_terms([(p, 0) for p in early])
@@ -342,7 +420,7 @@
     half = (z // 2 + y_hi) % 2
 
     def place_update(p):
-        cross_out[span(p), :] = sum_update(p, 1)
+        cross_out[span(p), :] = sum_update(p, 1).astype(BF16)
         cross(p).start()
         out[span(p), pl.ds(pl.multiple_of(half * quarter, quarter), quarter)] = sum_update(p, 0)
 
@@ -373,10 +451,11 @@
     place_update(PARTS - 1)
     for p in range(PARTS):
         cross(p).wait_recv()
-        out[span(p), pl.ds(pl.multiple_of((1 - half) * quarter, quarter), quarter)] = cross_in[span(p), :]
+        out[span(p), pl.ds(pl.multiple_of((1 - half) * quarter, quarter), quarter)] = cross_in[span(p), :].astype(F32)
 
     for j in range(SIDES):
-        spread_sent(g_in.at[:, half_of(j)], g_all.at[row, :, half_of(j)], g_s.at[j], g_r.at[j])
+        g_sent(j)
+        g_relayed(j)
     for step in (1, 3):
         for bit in range(2):
             along_x(step, bit).wait_send()
@@ -420,12 +499,12 @@
             pltpu.VMEM((3, 2, height, in_factor.shape[1]), BF16),
             pltpu.VMEM((2, height, in_factor.shape[1]), F32),
             pltpu.VMEM((3, 2, height, in_factor.shape[1]), BF16),
-            pltpu.VMEM((height, in_factor.shape[1]), F32),
-            pltpu.VMEM((height, in_factor.shape[1]), F32),
+            pltpu.VMEM((height, in_factor.shape[1]), BF16),
+            pltpu.VMEM((height, in_factor.shape[1]), BF16),
             dma((LOADS,)), dma((LOADS,)),
             dma((LOADS, 3)), dma((LOADS, 3)),
             dma((LOADS, 4)), dma((LOADS, 4)),
-            dma((SIDES, 4)), dma((SIDES, 4)),
+            dma((SIDES, 2, 3)), dma((SIDES, 4, 2)), dma((SIDES, 2, 2)),
             dma((2,)), dma((2,)),
             dma((3, 2)), dma((3, 2)),
             dma((4,)), dma((4,)),

time: 183 us -> 176 us (0.962)
  Pallas kernels: 177 us -> 170 us
    pallas_call x1, Pallas kernels: 177 us -> 170 us  [shards(): pl.pallas_call(kernel, out_shape=jax.ShapeDtypeStruct((height, width), F3...]
where the time goes in v5:
time: 176 us; the launch traced here: 173 us
  Pallas kernels  170 us (97%)
  local copies, waits for them, and re-layouts  3.16 us (2%)
    pallas_call x1, Pallas kernels, shards(): pl.pallas_call(kernel, out_shape=jax.ShapeDtypeStruct((height, width), F3...  170 us

profile of v5, /device:TPU:1, one launch (start us, length us, event | category | flops | bytes accessed | tf_op | source)
XLA Modules:
  0.0 172.9 jit_solution(17262627310957742467)
XLA Ops:
  0.0 169.7 %shard_map.37 = f32[512,1024]{1,0:T(8,128)} custom-call(bf16[4,512,256]{2,1,0:T(8,128)(2,1)} %bitcast.1, bf16[512,1024]{1,0:T(8,128)(2,1)} %g_in.1, bf16[1024,512]{1,0:T(8,128)(2,1)} %b_in.1), custom_call_target="tpu_custom_call" | custom-call | flops 34359738368 | bytes 8388608 | tf_op jit(solution)/shard_map/pallas_call | solution.py:484
  169.7 3.2 %copy.5 = f32[512,1024]{1,0:T(8,128)} copy(f32[512,1024]{1,0:T(8,128)} %shard_map.37) | data formatting | bytes 4194304

commit v6 on v5

--- a/solution.py
+++ b/solution.py
@@ -19,7 +19,7 @@
     return ((y // 2) * 2 + core, (y % 2) * 4 + z, x)
 
 
-def kernel(a_in, g_in, b_in, out, a_all, g_all, b_all, terms, terms_in, far, far_in, own_h, h_all, u_out, u_own, u_in, cross_out, cross_in,
+def kernel(a_in, g_in, b_in, out, a_all, g_all, b_all, terms, terms_in, far, far_in, near, near_in, own_h, h_all, u_out, u_own, u_in, cross_out, cross_in,
            swap_s, swap_r, az_s, az_r, ac_s, ac_r, g_s, g_r, f_s, turn_s, turn_r, bx_s, bx_r, bc_s, bc_r,
            t_s, t_r, h_s, h_r, u_s, u_r, c_s, c_r):
     row, col, x = lax.axis_index("row"), lax.axis_index("col"), lax.axis_index("depth")
@@ -281,8 +281,10 @@
         block = (span(p), half_of(j))
         if step == 2:
             src, dst, to = far.at[block], far_in.at[block], relay(j)
+        elif step != relay(j):
+            src, dst, to = near.at[block], near_in.at[block], step
         else:
-            src, dst, to = terms.at[(step // 2 + 1,) + block], terms_in.at[(step // 2,) + block], step
+            src, dst, to = terms.at[(1,) + block], terms_in.at[block], step
         return remote(src, dst, t_s.at[p, j, step - 1], t_r.at[p, j, step - 1], place((x + to) % 4, y, z, core))
 
     def relay(j):
@@ -328,9 +330,11 @@
             if step == 2:
                 far[span(p), columns] = product.astype(BF16)
             elif step == relay(j):
-                terms[(step + 1) // 2, span(p), columns] = product + far_in[span(p), columns].astype(F32)
+                terms[1, span(p), columns] = product + far_in[span(p), columns].astype(F32)
+            elif step == 0:
+                terms[0, span(p), columns] = product
             else:
-                terms[(step + 1) // 2, span(p), columns] = product
+                near[span(p), columns] = product.astype(BF16)
             return 0
 
         lax.fori_loop(0, side // TILE, tile, 0)
@@ -384,9 +388,7 @@
         for j in range(SIDES):
             for step in (1, 3):
                 give(p, j, step).wait_recv()
-        total = terms[0, span(p), :]
-        for step in range(2):
-            total += terms_in[step, span(p), :]
+        total = terms[0, span(p), :] + terms_in[span(p), :] + near_in[span(p), :].astype(F32)
         own_h[span(p), :] = total.astype(BF16)
         spread_start(own_h.at[span(p), :], h_all.at[row, span(p), :], h_s.at[p], h_r.at[p])
 
@@ -420,7 +422,7 @@
     half = (z // 2 + y_hi) % 2
 
     def place_update(p):
-        cross_out[span(p), :] = sum_update(p, 1).astype(BF16)
+        cross_out[span(p), :] = sum_update(p, 1)
         cross(p).start()
         out[span(p), pl.ds(pl.multiple_of(half * quarter, quarter), quarter)] = sum_update(p, 0)
 
@@ -451,7 +453,7 @@
     place_update(PARTS - 1)
     for p in range(PARTS):
         cross(p).wait_recv()
-        out[span(p), pl.ds(pl.multiple_of((1 - half) * quarter, quarter), quarter)] = cross_in[span(p), :].astype(F32)
+        out[span(p), pl.ds(pl.multiple_of((1 - half) * quarter, quarter), quarter)] = cross_in[span(p), :]
 
     for j in range(SIDES):
         g_sent(j)
@@ -490,8 +492,10 @@
             pltpu.VMEM((8, 4, height, out_factor.shape[1]), BF16),
             pltpu.VMEM((4, height, width), BF16),
             pltpu.VMEM((2, 4) + in_factor.shape, BF16),
-            pltpu.VMEM((3, height, width), F32),
             pltpu.VMEM((2, height, width), F32),
+            pltpu.VMEM((height, width), F32),
+            pltpu.VMEM((height, width), BF16),
+            pltpu.VMEM((height, width), BF16),
             pltpu.VMEM((height, width), BF16),
             pltpu.VMEM((height, width), BF16),
             pltpu.VMEM((height, width), BF16),
@@ -499,8 +503,8 @@
             pltpu.VMEM((3, 2, height, in_factor.shape[1]), BF16),
             pltpu.VMEM((2, height, in_factor.shape[1]), F32),
             pltpu.VMEM((3, 2, height, in_factor.shape[1]), BF16),
-            pltpu.VMEM((height, in_factor.shape[1]), BF16),
-            pltpu.VMEM((height, in_factor.shape[1]), BF16),
+            pltpu.VMEM((height, in_factor.shape[1]), F32),
+            pltpu.VMEM((height, in_factor.shape[1]), F32),
             dma((LOADS,)), dma((LOADS,)),
             dma((LOADS, 3)), dma((LOADS, 3)),
             dma((LOADS, 4)), dma((LOADS, 4)),

time: 176 us -> 178 us (1.011)
  Pallas kernels: 170 us -> 172 us
    pallas_call x1, Pallas kernels: 170 us -> 172 us  [shards(): pl.pallas_call(kernel, out_shape=jax.ShapeDtypeStruct((height, width), F3...]
where the time goes in v6:
time: 178 us; the launch traced here: 175 us
  Pallas kernels  172 us (97%)
  local copies, waits for them, and re-layouts  3.16 us (2%)
    pallas_call x1, Pallas kernels, shards(): pl.pallas_call(kernel, out_shape=jax.ShapeDtypeStruct((height, width), F3...  172 us

profile of v6, /device:TPU:1, one launch (start us, length us, event | category | flops | bytes accessed | tf_op | source)
XLA Modules:
  0.0 175.3 jit_solution(9269404091290695004)
XLA Ops:
  0.0 172.1 %shard_map.37 = f32[512,1024]{1,0:T(8,128)} custom-call(bf16[4,512,256]{2,1,0:T(8,128)(2,1)} %bitcast.1, bf16[512,1024]{1,0:T(8,128)(2,1)} %g_in.1, bf16[1024,512]{1,0:T(8,128)(2,1)} %b_in.1), custom_call_target="tpu_custom_call" | custom-call | flops 34359738368 | bytes 8388608 | tf_op jit(solution)/shard_map/pallas_call | solution.py:486
  172.1 3.2 %copy.5 = f32[512,1024]{1,0:T(8,128)} copy(f32[512,1024]{1,0:T(8,128)} %shard_map.37) | data formatting | bytes 4194304

commit v7 on v5

--- a/solution.py
+++ b/solution.py
@@ -313,9 +313,8 @@
         for step in (2, 1, 3):
             along_z(p, step).start()
         across_a(p, 0).start()
+        g_start(p)
     across_b(0).start()
-    for j in range(SIDES):
-        g_start(j)
 
     def first_product(p, j, step):
         owner = (x + step) % 4

time: 176 us -> 176 us (level)
  no operation moved by 1% of the time
where the time goes in v7:
time: 176 us; the launch traced here: 173 us
  Pallas kernels  170 us (97%)
  local copies, waits for them, and re-layouts  3.16 us (2%)
    pallas_call x1, Pallas kernels, shards(): pl.pallas_call(kernel, out_shape=jax.ShapeDtypeStruct((height, width), F3...  170 us

profile of v7, /device:TPU:1, one launch (start us, length us, event | category | flops | bytes accessed | tf_op | source)
XLA Modules:
  0.0 172.9 jit_solution(562704006400279221)
XLA Ops:
  0.0 169.8 %shard_map.37 = f32[512,1024]{1,0:T(8,128)} custom-call(bf16[4,512,256]{2,1,0:T(8,128)(2,1)} %bitcast.1, bf16[512,1024]{1,0:T(8,128)(2,1)} %g_in.1, bf16[1024,512]{1,0:T(8,128)(2,1)} %b_in.1), custom_call_target="tpu_custom_call" | custom-call | flops 34359738368 | bytes 8388608 | tf_op jit(solution)/shard_map/pallas_call | solution.py:483
  169.8 3.2 %copy.5 = f32[512,1024]{1,0:T(8,128)} copy(f32[512,1024]{1,0:T(8,128)} %shard_map.37) | data formatting | bytes 4194304
